TPU v7x, 32 devices: a whole 2x2x4 slice. The times are simulated.
32 devices in a mesh: dp: 8 (over z, x), section: 4 (over y, core).
Axes of the slice: x: 2, y: 2, z: 4, core: 2. Of those that a mesh axis runs over, the one named last changes fastest.
Arguments:
- images_in: bfloat16 [2048, 4096], P(('dp', 'section')), may hold values from -6 to 6
- labels: int32 [2048], P(('dp', 'section')), may hold values from 0 to 9
- conv_weight: float32 [3, 2, 576, 64], P(None, None, None, 'section'), may hold values from -0.25 to 0.25
- frn_gain: float32 [3, 2, 64], replicated, may hold values from 0.25 to 1.75
- frn_bias: float32 [3, 2, 64], replicated, may hold values from -3 to 3
- head_weight: float32 [64, 10], replicated, as said below
- head_bias: float32 [10], replicated, may hold values from -4 to 4
Outputs:
- grad_conv: float32 [3, 2, 576, 64], P(None, None, None, 'section')
- grad_norm: float32 [3, 2, 2, 64], replicated
- grad_head_weight: float32 [64, 10], replicated
- grad_head_bias: float32 [10], replicated
Inputs may be any that keep to these rules, and one draw needn't show every extreme that they name: `head_weight`: the classifier's weights.
All inputs are finite; a program needn't handle non-finite values.
Results may differ from a plain program's by a relative error of at most 0.0033.
The roundings to bfloat16 on the way count: a program that leaves them out, or rounds other values in their place, can miss the bound.
Values may be sent and summed in bfloat16 or wider, within the bound.
A program may use at most 64 MiB of HBM per device.

v0:
```python
import functools

import jax
import jax.numpy as jnp
from jax import lax
from jax.experimental import pallas as pl
from jax.experimental.pallas import tpu as pltpu
from jax.sharding import PartitionSpec as P

F32 = jnp.float32
BF16 = jnp.bfloat16
MESH = pl.DeviceIdType.MESH
eps = 1e-06
prior_precision = 0.5
OFFSETS = (0, 1, 2, -1)


CHUNKS = ((5, 4), (3, 2), (1,), (0,))


def chunk_tiles(c):
    return 9 * len(CHUNKS[c]) + (3 if c == 0 else 1)


def kernel(total, dps, secs, img_hbm, labels, own_hbm, gain, bias, hw, hb, conv_out, small,
           xs, zs, dsw, rs, wf, wb, qs, qt, du2, du1, hw2, lab, wt, buf, in_a, tot, in_b,
           fin, img, own, load, w_send, w_recv, a_send, a_recv, b_send, b_recv, c_send, c_recv):
    dp, sec = lax.axis_index("dp"), lax.axis_index("section")
    per = [-(-chunk_tiles(c) // dps) for c in range(len(CHUNKS))]

    load_own = pltpu.make_async_copy(own_hbm, own, load.at[0])
    load_img = pltpu.make_async_copy(img_hbm, img, load.at[1])
    load_own.start()
    load_img.start()
    barrier = pltpu.get_barrier_semaphore()
    for d in range(1, secs):
        pl.semaphore_signal(barrier, inc=1, device_id=(dp, lax.rem(sec + d, secs)),
                            device_id_type=MESH)

    def greet(d, carry):
        pl.semaphore_signal(barrier, inc=1, device_id=(lax.rem(dp + d, dps), sec),
                            device_id_type=MESH)
        return carry

    lax.fori_loop(1, dps, greet, 0)
    load_own.wait()
    wt[sec] = own[...].astype(BF16)
    pl.semaphore_wait(barrier, secs - 1 + dps - 1)

    def send_w(b, d):
        mine = wt.at[sec, pl.ds(2 * b, 2)]
        return pltpu.make_async_remote_copy(
            src_ref=mine, dst_ref=mine, send_sem=w_send.at[b, d - 1],
            recv_sem=w_recv.at[b, d - 1], device_id=(dp, lax.rem(sec + d, secs)),
            device_id_type=MESH)

    def send_a(b, d):
        to = lax.rem(sec + d, secs)
        return pltpu.make_async_remote_copy(
            src_ref=buf.at[b, to, pl.ds(0, chunk_tiles(b))],
            dst_ref=in_a.at[b, d - 1, pl.ds(0, chunk_tiles(b))], send_sem=a_send.at[b, d - 1],
            recv_sem=a_recv.at[b, d - 1], device_id=(dp, to), device_id_type=MESH)

    def send_b(b, d):
        to = lax.rem(dp + d, dps)
        return pltpu.make_async_remote_copy(
            src_ref=tot.at[b, pl.ds(to * per[b], per[b])],
            dst_ref=in_b.at[b, d - 1, pl.ds(0, per[b])],
            send_sem=b_send.at[b, d - 1], recv_sem=b_recv.at[b, d - 1],
            device_id=(to, sec), device_id_type=MESH)

    def send_c(b, d):
        to = lax.rem(dp + d, dps)
        mine = fin.at[b, pl.ds(dp * per[b], per[b])]
        return pltpu.make_async_remote_copy(
            src_ref=mine, dst_ref=mine, send_sem=c_send.at[b, d - 1],
            recv_sem=c_recv.at[b, d - 1], device_id=(to, sec), device_id_type=MESH)

    def each_dp(act):
        def step(d, carry):
            act(d)
            return carry
        lax.fori_loop(1, dps, step, 0)

    def start_a(b):
        for d in range(1, secs):
            send_a(b, d).start()

    def start_b(b):
        for d in range(1, secs):
            send_a(b, d).wait_recv()
        tiles = chunk_tiles(b)
        all_terms = buf[b, sec, 0:tiles]
        for d in range(1, secs):
            all_terms = all_terms + in_a[b, d - 1, 0:tiles]
        tot[b, 0:tiles] = all_terms
        if tot.shape[1] > tiles:
            tot[b, tiles:] = jnp.zeros((tot.shape[1] - tiles, 8, 128), F32)
        each_dp(lambda d: send_b(b, d).start())

    def start_c(b):
        each_dp(lambda d: send_b(b, d).wait_recv())
        sums = lax.fori_loop(1, dps, lambda d, acc: acc + in_b[b, d - 1, 0:per[b]],
                             tot[b, pl.ds(dp * per[b], per[b])])
        fin[b, pl.ds(dp * per[b], per[b])] = sums
        each_dp(lambda d: send_c(b, d).start())

    def end_c(b):
        each_dp(lambda d: send_c(b, d).wait_recv())

    for b in range(3):
        for d in range(1, secs):
            send_w(b, d).start()
    lane = lax.broadcasted_iota(jnp.int32, (1, 128), 1)
    low = lane < 64

    def both(v):
        return v + pltpu.roll(v, 64, 1)

    def twice(v):
        return jnp.concatenate([v, v], axis=1)

    for ref in (qs, qt):
        ref[0] = jnp.zeros(ref.shape[1:], BF16)
        ref[9] = jnp.zeros(ref.shape[1:], BF16)
    for k in range(6):
        xs[k, 0] = jnp.zeros((256, 256), BF16)
        xs[k, 9] = jnp.zeros((256, 256), BF16)

    def put(ref, y, v):
        edge = jnp.zeros((1, 64, 128), F32)
        after = jnp.concatenate([v[1:], edge], axis=0)
        before = jnp.concatenate([edge, v[:3]], axis=0)
        beside = jnp.where(low[None], after, before)
        ref[y + 1, :, 0:128] = v.reshape(256, 128).astype(BF16)
        ref[y + 1, :, 128:256] = beside.reshape(256, 128).astype(BF16)

    def conv(src, w, body, init):
        def step(y2, carry):
            rows = jnp.concatenate([src[2 * y2 + r] for r in range(4)], axis=1)
            out = jnp.dot(rows, w[...], preferred_element_type=F32)
            for yo in range(2):
                carry = body(2 * y2 + yo, out[:, yo * 128:yo * 128 + 128], carry)
            return carry
        return lax.fori_loop(0, 4, step, init)

    zero_sum = jnp.zeros((64, 128), F32)

    def over_pairs(v):
        return jnp.sum(v.reshape(4, 64, 128), axis=0)

    load_img.wait()
    for y in range(8):
        slab = jnp.stack([img[:, (y * 4 + j) * 128:(y * 4 + j + 1) * 128]
                          for j in range(4)], axis=0).astype(F32)
        put(xs.at[0], y, slab)

    def spread(b):
        for d in range(1, secs):
            send_w(b, d).wait_recv()
        flat = jnp.concatenate(
            [wt[q, 2 * b + j] for j in range(2) for q in range(secs)], axis=0).astype(F32)
        zero = jnp.zeros((64, 128), BF16)
        cols = jnp.concatenate([flat, jnp.zeros((128, 64), F32)], axis=1).T
        plain = [cols[t * 64:(t + 1) * 64] for t in range(9)]
        turned = [pltpu.roll(v, 64, 1) for v in plain]
        none = jnp.zeros((64, 128), F32)
        for j in range(2):
            first, second = (plain, turned) if j == 0 else (turned, plain)
            for a in range(3):
                for s, xi in enumerate(OFFSETS):
                    left = first[a * 3 + xi + 1] if 0 <= xi + 1 <= 2 else none
                    right = second[a * 3 + xi] if 0 <= xi <= 2 else none
                    tile = jnp.where(low, left, right).astype(BF16)
                    for yo in range(2):
                        row = (a + yo) * 256 + s * 64
                        wf[2 * b + j, row:row + 64, yo * 128:yo * 128 + 128] = tile
        wide = jnp.concatenate(
            [jnp.zeros((128, 64), F32), flat, jnp.zeros((128, 128), F32)], axis=1)
        for a in range(3):
            for s, xi in enumerate(OFFSETS):
                at = ((2 - a) * 3 + 2 - xi) * 64
                tile = wide[:, at:at + 128]
                if xi == -1:
                    tile = jnp.where(low, tile, 0.0)
                if xi == 2:
                    tile = jnp.where(low, 0.0, tile)
                tile = tile.astype(BF16)
                for j in range(2):
                    for yo in range(2):
                        row = (a + yo) * 256 + s * 64
                        wb[2 * b + j, row:row + 64, yo * 128:yo * 128 + 128] = (
                            tile[j * 64:j * 64 + 64])
        for j in range(2):
            for ref in (wf, wb):
                for s in range(4):
                    ref[2 * b + j, 768 + s * 64:832 + s * 64, 0:128] = zero
                    ref[2 * b + j, s * 64:s * 64 + 64, 128:256] = zero

    pooled = zero_sum
    for k in range(6):
        b, j = k // 2, k % 2
        if j == 0:
            spread(b)

        def keep(y, out, energy):
            zs[k, y] = out
            return energy + over_pairs(out * out)

        energy = conv(xs.at[k], wf.at[k], keep, zero_sum)
        r = lax.rsqrt(both(energy) * (1.0 / 64) + eps)
        rs[k] = r
        scale = r * twice(gain[b, j:j + 1, :])
        shift = twice(bias[b, j:j + 1, :])

        def activate(y, carry):
            u = zs[k, y].reshape(4, 64, 128) * scale[None] + shift[None]
            if j == 1:
                u = u + xs[k - 1, y + 1, :, 0:128].astype(F32).reshape(4, 64, 128)
            sig = 0.5 * jnp.tanh(0.5 * u) + 0.5
            out = u * sig
            dsw[k, y] = (sig + out * (1.0 - sig)).reshape(256, 128)
            if k < 5:
                put(xs.at[k + 1], y, out)
                return carry
            return carry + jnp.sum(out.astype(BF16).astype(F32), axis=0)

        pooled = lax.fori_loop(0, 8, activate, pooled)

    pooled = both(pooled) * (1.0 / 64)
    hw2[...] = jnp.zeros((128, 128), F32)
    hw2[0:hw.shape[0], :] = twice(hw[...])
    lab[...] = jnp.zeros((8, 128), jnp.int32)
    lab[0:1, 0:64] = labels[...]
    classes = hw.shape[0]
    hbias = jnp.concatenate([hb[...], jnp.zeros((1, 128 - classes), F32)], axis=1)
    logits = lax.dot_general(jnp.where(low, pooled, 0.0), hw2[...],
                             (((1,), (1,)), ((), ())), precision=lax.Precision.HIGHEST,
                             preferred_element_type=F32) + hbias
    live = lane < classes
    logits = jnp.where(live, logits, -1e30)
    top = jnp.max(logits, axis=1, keepdims=True)
    expo = jnp.where(live, jnp.exp(logits - top), 0.0)
    probs = expo / jnp.sum(expo, axis=1, keepdims=True)
    onehot = jnp.where(
        lax.broadcasted_iota(jnp.int32, (128, 128), 0) == lab[0:1, :], 1.0, 0.0).T
    dl = (probs - onehot[0:64]) * (1.0 / total)
    dlt = jnp.concatenate([dl, jnp.zeros((64, 128), F32)], axis=0).T
    tall = jnp.concatenate([pooled, jnp.zeros((64, 128), F32)], axis=0)
    d_head = jnp.dot(dlt[0:16], tall, precision=lax.Precision.HIGHEST,
                     preferred_element_type=F32)
    row = lax.broadcasted_iota(jnp.int32, (8, 128), 0)
    extra = jnp.where(row == 4, jnp.sum(dl, axis=0, keepdims=True), 0.0)
    for q in range(secs):
        buf[0, q, 19] = d_head[0:8]
        buf[0, q, 20] = d_head[8:16]
    spread_g = jnp.dot(dl, hw2[...], precision=lax.Precision.HIGHEST,
                       preferred_element_type=F32) * (1.0 / 64)
    spread_g = spread_g.astype(BF16).astype(F32)

    def tally(k, y, d, sums):
        return (sums[0] + over_pairs(d * zs[k, y]), sums[1] + over_pairs(d))

    def begin(y, sums):
        d = (dsw[5, y].reshape(4, 64, 128) * spread_g[None]).reshape(256, 128)
        du2[y] = d
        return tally(5, y, d, sums)

    sums = lax.fori_loop(0, 8, begin, (zero_sum, zero_sum))
    for k in range(5, -1, -1):
        b, j = k // 2, k % 2
        source = du2 if j == 1 else du1
        c = [k in ks for ks in CHUNKS].index(True)
        at_tile = CHUNKS[c].index(k)
        ends = k == CHUNKS[c][-1]
        r = rs[k]
        dg = both(sums[0]) * r
        db = both(sums[1])
        extra = jnp.where(row == 2 * at_tile, jnp.sum(dg, axis=0, keepdims=True), extra)
        extra = jnp.where(row == 2 * at_tile + 1, jnp.sum(db, axis=0, keepdims=True), extra)
        if ends:
            for q in range(secs):
                buf[c, q, 9 * len(CHUNKS[c])] = extra
            extra = jnp.zeros((8, 128), F32)
        c1 = r * twice(gain[b, j:j + 1, :])
        c2 = c1 * dg * r * (1.0 / 64)

        def settle(y, carry):
            d = (source[y].reshape(4, 64, 128) * c1[None]
                 - zs[k, y].reshape(4, 64, 128) * c2[None])
            if k > 0:
                put(qs, y, d)
            qt[y + 1] = d.reshape(256, 128).T.astype(BF16)
            return carry

        lax.fori_loop(0, 8, settle, 0)

        left = jnp.concatenate(
            [jnp.concatenate([qt[y - a + 2] for y in range(8)], axis=1) for a in range(3)],
            axis=0)
        right = jnp.concatenate([xs[k, y + 1] for y in range(8)], axis=0)
        terms = jnp.dot(left, right, preferred_element_type=F32)
        for a in range(3):
            zero_side = pltpu.roll(terms[a * 128:a * 128 + 64], 64, 1)
            both_sides = zero_side + terms[a * 128 + 64:a * 128 + 128]
            for e in range(3):
                at = e // 2 * 128
                here = both_sides[:, at:at + 128]
                there = pltpu.roll(here, 64, 1)
                first, second = (here, there) if e % 2 == 0 else (there, here)
                for q in range(secs):
                    buf[c, q, at_tile * 9 + a * 3 + e] = jnp.where(
                        low, first[q * 16:q * 16 + 8], second[q * 16 + 8:q * 16 + 16])

        if ends:
            start_a(c)
        if k == 3:
            start_b(0)
        if k == 2:
            start_c(0)

        if j == 1:
            def to_first(y, out, sums):
                d = out * dsw[k - 1, y]
                du1[y] = d
                return tally(k - 1, y, d, sums)

            sums = conv(qs, wb.at[k], to_first, (zero_sum, zero_sum))
            if k == 1:
                start_b(1)
        elif k > 0:
            def to_second(y, out, sums):
                g = (du2[y] + out).astype(BF16).astype(F32)
                d = g * dsw[k - 1, y]
                du2[y] = d
                return tally(k - 1, y, d, sums)

            sums = conv(qs, wb.at[k], to_second, (zero_sum, zero_sum))

    start_c(1)
    start_b(2)
    start_b(3)
    start_c(2)
    start_c(3)
    for c, ks in enumerate(CHUNKS):
        end_c(c)
        for at_tile, k in enumerate(ks):
            rows = [fin[c, at_tile * 9 + t] for t in range(9)]
            conv_out[k, 0:8] = jnp.concatenate([v[:, 0:64] for v in rows], axis=1)
            conv_out[k, 8:16] = jnp.concatenate([v[:, 64:128] for v in rows], axis=1)
            small[2 * k:2 * k + 2] = fin[c, 9 * len(ks)][2 * at_tile:2 * at_tile + 2]
        if c == 0:
            small[12:13] = fin[c, 18][4:5]
            small[16:24] = fin[c, 19]
            small[24:32] = fin[c, 20]
    for b in range(3):
        for d in range(1, secs):
            send_w(b, d).wait_send()
    for c in range(len(CHUNKS)):
        for d in range(1, secs):
            send_a(c, d).wait_send()
        each_dp(lambda d: send_b(c, d).wait_send())
        each_dp(lambda d: send_c(c, d).wait_send())


def all_grads(total, dps, secs, images_in, labels, own, gain, bias, hw, hb):
    vmem = pl.BlockSpec(memory_space=pltpu.VMEM)
    chunks = len(CHUNKS)
    tiles = max(chunk_tiles(c) for c in range(chunks))
    per = -(-tiles // dps)
    hbm = pl.BlockSpec(memory_space=pltpu.HBM)
    dma = pltpu.SemaphoreType.DMA
    return pl.pallas_call(
        functools.partial(kernel, total, dps, secs),
        out_shape=(jax.ShapeDtypeStruct(own.shape, F32),
                   jax.ShapeDtypeStruct((32, 128), F32)),
        in_specs=[hbm, vmem, hbm, vmem, vmem, vmem, vmem],
        out_specs=(vmem, vmem),
        scratch_shapes=[
            pltpu.VMEM((6, 10, 256, 256), BF16),
            pltpu.VMEM((6, 8, 256, 128), F32),
            pltpu.VMEM((6, 8, 256, 128), F32),
            pltpu.VMEM((6, 64, 128), F32),
            pltpu.VMEM((6, 1024, 256), BF16),
            pltpu.VMEM((6, 1024, 256), BF16),
            pltpu.VMEM((10, 256, 256), BF16),
            pltpu.VMEM((10, 128, 256), BF16),
            pltpu.VMEM((8, 256, 128), F32),
            pltpu.VMEM((8, 256, 128), F32),
            pltpu.VMEM((128, 128), F32),
            pltpu.VMEM((8, 128), jnp.int32),
            pltpu.VMEM((secs,) + own.shape, BF16),
            pltpu.VMEM((chunks, secs, tiles, 8, 128), F32),
            pltpu.VMEM((chunks, secs - 1, tiles, 8, 128), F32),
            pltpu.VMEM((chunks, per * dps, 8, 128), F32),
            pltpu.VMEM((chunks, dps - 1, per, 8, 128), F32),
            pltpu.VMEM((chunks, per * dps, 8, 128), F32),
            pltpu.VMEM(images_in.shape, BF16),
            pltpu.VMEM(own.shape, F32),
            dma((2,)),
            dma((3, secs - 1)), dma((3, secs - 1)),
            dma((chunks, secs - 1)), dma((chunks, secs - 1)),
            dma((chunks, dps - 1)), dma((chunks, dps - 1)),
            dma((chunks, dps - 1)), dma((chunks, dps - 1)),
        ],
        compiler_params=pltpu.CompilerParams(
            vmem_limit_bytes=63 * 1024 * 1024 + 768 * 1024, collective_id=0, has_side_effects=True),
    )(images_in, labels, own, gain, bias, hw, hb)


def per_device(images_in, labels, conv_weight, frn_gain, frn_bias, head_weight, head_bias):
    images = images_in.shape[0]
    dps, secs = lax.axis_size("dp"), lax.axis_size("section")
    blocks, convs, depth, share = conv_weight.shape
    own = jnp.swapaxes(conv_weight, 2, 3).reshape(blocks * convs, share, depth)
    owned, small = all_grads(images * dps * secs, dps, secs, images_in,
                             labels.reshape(1, images), own, frn_gain,
                             frn_bias, head_weight.T, head_bias.reshape(1, -1))
    classes = head_bias.shape[0]
    params = jnp.stack([frn_gain, frn_bias], axis=2)
    return (
        jnp.swapaxes(owned.reshape(blocks, convs, share, depth), 2, 3)
        + prior_precision * conv_weight,
        small[0:12, 0:64].reshape(params.shape)
        + prior_precision * params,
        small[16:16 + classes, 0:64].T + prior_precision * head_weight,
        small[12, 0:classes] + prior_precision * head_bias,
    )


def solution(mesh):
    return jax.shard_map(
        per_device,
        mesh=mesh,
        in_specs=(
            P(("dp", "section"), None),
            P(("dp", "section")),
            P(None, None, None, "section"),
            P(),
            P(),
            P(),
            P(),
        ),
        out_specs=(P(None, None, None, "section"), P(), P(), P()),
        check_vma=False,
    )
```

profile of v0, /device:TPU:0, one launch (start us, length us, event | category | flops | bytes accessed | tf_op | source)
XLA Modules:
  0.0 65.7 jit_solution(4855034968180427687)
XLA Ops:
  0.6 60.6 %shard_map.102 = (f32[6,16,576]{2,1,0:T(8,128)}, f32[32,128]{1,0:T(8,128)}) custom-call(bf16[64,4096]{1,0:T(8,128)(2,1)} %img_hbm.1, s32[1,64]{1,0:T(1,128)} %bitcast.20, f32[6,16,576]{2,1,0:T(8,128)} %bitcast.15, f32[3,2,64]{2,1,0:T(2,128)} %gain.1, f32[3,2,64]{2,1,0:T(2,128)} %bias.1, f32[10,64]{1,0:T(8,128)} %bitcast.17, f32[1,10]{1,0:T(1,128)} %bitcast.21), custom_call_target="tpu_custom_call" | custom-call | tf_op jit(solution)/shard_map/pallas_call | solution.py:373
  61.2 0.0 copy-start.2
  61.2 0.0 copy-start.3
  61.3 0.7 %slice.9 = f32[12,64]{1,0:T(8,128)S(1)} slice(f32[32,128]{1,0:T(8,128)} %get-tuple-element.7), slice={[0:12], [0:64]} | slice | bytes 6144 | tf_op jit(solution)/shard_map/slice | solution.py:424
  62.0 0.0 copy-start.1
  62.0 0.0 copy-done.2
  62.0 0.0 copy-done.3
  62.0 0.0 copy-start
  62.0 0.6 fusion
  62.6 0.1 copy-done.1
  62.7 0.0 copy-done
  62.7 0.0 copy-start.4
  62.7 0.6 bitcast_add_fusion
  63.3 0.1 copy-done.4
  63.4 0.5 bitcast_add_fusion.1
  63.9 1.8 %multiply_add_fusion = f32[3,2,576,16]{2,3,1,0:T(8,128)} fusion(f32[3,2,576,16]{2,3,1,0:T(8,128)} %bitcast.16, f32[3,2,576,16]{2,3,1,0:T(8,128)} %param.9), kind=kLoop, calls=%fused_computation | loop fusion | flops 110592 | bytes 663552 | tf_op jit(solution)/shard_map/add | solution.py:422
  (1 shorter events, 0.0 us)
Async XLA Ops:
  61.2 0.7 %copy-start.2 = (f32[3,2,64]{2,1,0:T(2,128)S(1)}, f32[3,2,64]{2,1,0:T(2,128)}, u32[]{:S(2)}) copy-start(f32[3,2,64]{2,1,0:T(2,128)} %gain.1) | copy-start | bytes 4612
  61.2 0.7 %copy-start.3 = (f32[3,2,64]{2,1,0:T(2,128)S(1)}, f32[3,2,64]{2,1,0:T(2,128)}, u32[]{:S(2)}) copy-start(f32[3,2,64]{2,1,0:T(2,128)} %bias.1) | copy-start | bytes 4612
  62.0 0.7 %copy-start.1 = (f32[32,128]{1,0:T(8,128)S(1)}, f32[32,128]{1,0:T(8,128)}, u32[]{:S(2)}) copy-start(f32[32,128]{1,0:T(8,128)} %get-tuple-element.7) | copy-start | bytes 49156
  62.0 0.7 %copy-start = (f32[64,10]{0,1:T(8,128)S(1)}, f32[64,10]{0,1:T(8,128)}, u32[]{:S(2)}) copy-start(f32[64,10]{0,1:T(8,128)} %param.12) | copy-start | bytes 7684
  62.7 0.7 %copy-start.4 = (f32[10]{0:T(128)S(1)}, f32[10]{0:T(128)}, u32[]{:S(2)}) copy-start(f32[10]{0:T(128)} %param.13) | copy-start | bytes 124
where the time goes:
time: 66 us; the launch traced here: 65.7 us
  Pallas kernels  60.6 us (92%)
  other arithmetic  3.5 us (5%)
  local copies, waits for them, and re-layouts  0.87 us (1%)
  between operations  0.68 us (1%)
    pallas_call x1, Pallas kernels, all_grads(): pl.pallas_call(functools.partial(kernel, total, dps, secs), out_shape=(ja...  60.6 us
    add x1, other arithmetic, per_device(): jnp.swapaxes(owned.reshape(blocks, convs, share, depth), 2, 3)  1.78 us

commit v1 on v0

--- a/solution.py
+++ b/solution.py
@@ -136,13 +136,38 @@
         ref[y + 1, :, 128:256] = beside.reshape(256, 128).astype(BF16)
 
     def conv(src, w, body, init):
-        def step(y2, carry):
-            rows = jnp.concatenate([src[2 * y2 + r] for r in range(4)], axis=1)
-            out = jnp.dot(rows, w[...], preferred_element_type=F32)
-            for yo in range(2):
-                carry = body(2 * y2 + yo, out[:, yo * 128:yo * 128 + 128], carry)
+        def run(*accs):
+            for m in range(2):
+                for kt in range(2):
+                    at = (2 * m + kt) * 256
+                    pltpu.matmul_push_rhs(w[at:at + 256, :], kt, m)
+            for kt in range(2):
+                for y2 in range(4):
+                    for m in range(2):
+                        pltpu.matmul_acc_lhs(accs[4 * m + y2], src[2 * y2 + 2 * m + kt],
+                                             load_staged_rhs=kt if y2 == 0 else None)
+            carry = init
+            for y2 in range(4):
+                out = pltpu.matmul_pop(accs[y2]) + pltpu.matmul_pop(accs[4 + y2])
+                for yo in range(2):
+                    carry = body(2 * y2 + yo, out[:, yo * 128:yo * 128 + 128], carry)
             return carry
-        return lax.fori_loop(0, 4, step, init)
+
+        return pl.run_scoped(run, *[pltpu.ACC(m)((256, 256), F32) for m in range(2) for _ in range(4)])
+
+    def split(v):
+        top = v.astype(BF16)
+        return [top, (v - top.astype(F32)).astype(BF16)]
+
+    def dot_f32(a, b):
+        def run(acc):
+            half = jnp.concatenate(split(b), axis=1)
+            pltpu.matmul_push_rhs(jnp.concatenate([half, half], axis=0), 0, 0)
+            pltpu.matmul_acc_lhs(acc, jnp.concatenate(split(a), axis=1), load_staged_rhs=0)
+            out = pltpu.matmul_pop(acc)
+            return out[:, 0:128] + out[:, 128:256]
+
+        return pl.run_scoped(run, pltpu.ACC(0)((a.shape[0], 256), F32))
 
     zero_sum = jnp.zeros((64, 128), F32)
 
@@ -234,9 +259,7 @@
     lab[0:1, 0:64] = labels[...]
     classes = hw.shape[0]
     hbias = jnp.concatenate([hb[...], jnp.zeros((1, 128 - classes), F32)], axis=1)
-    logits = lax.dot_general(jnp.where(low, pooled, 0.0), hw2[...],
-                             (((1,), (1,)), ((), ())), precision=lax.Precision.HIGHEST,
-                             preferred_element_type=F32) + hbias
+    logits = dot_f32(jnp.where(low, pooled, 0.0), hw2[...].T) + hbias
     live = lane < classes
     logits = jnp.where(live, logits, -1e30)
     top = jnp.max(logits, axis=1, keepdims=True)
@@ -247,15 +270,13 @@
     dl = (probs - onehot[0:64]) * (1.0 / total)
     dlt = jnp.concatenate([dl, jnp.zeros((64, 128), F32)], axis=0).T
     tall = jnp.concatenate([pooled, jnp.zeros((64, 128), F32)], axis=0)
-    d_head = jnp.dot(dlt[0:16], tall, precision=lax.Precision.HIGHEST,
-                     preferred_element_type=F32)
+    d_head = dot_f32(dlt[0:16], tall)
     row = lax.broadcasted_iota(jnp.int32, (8, 128), 0)
     extra = jnp.where(row == 4, jnp.sum(dl, axis=0, keepdims=True), 0.0)
     for q in range(secs):
         buf[0, q, 19] = d_head[0:8]
         buf[0, q, 20] = d_head[8:16]
-    spread_g = jnp.dot(dl, hw2[...], precision=lax.Precision.HIGHEST,
-                       preferred_element_type=F32) * (1.0 / 64)
+    spread_g = dot_f32(dl, hw2[...]) * (1.0 / 64)
     spread_g = spread_g.astype(BF16).astype(F32)
 
     def tally(k, y, d, sums):
@@ -295,11 +316,19 @@
 
         lax.fori_loop(0, 8, settle, 0)
 
-        left = jnp.concatenate(
-            [jnp.concatenate([qt[y - a + 2] for y in range(8)], axis=1) for a in range(3)],
-            axis=0)
-        right = jnp.concatenate([xs[k, y + 1] for y in range(8)], axis=0)
-        terms = jnp.dot(left, right, preferred_element_type=F32)
+        def weight_terms(*accs):
+            for step in range(4):
+                for m in range(2):
+                    y = 2 * step + m
+                    pltpu.matmul_push_rhs(xs[k, y + 1], step % 2, m)
+                    for a in range(3):
+                        pltpu.matmul_acc_lhs(accs[3 * m + a], qt[y - a + 2],
+                                             load_staged_rhs=step % 2 if a == 0 else None)
+            return jnp.concatenate(
+                [pltpu.matmul_pop(accs[a]) + pltpu.matmul_pop(accs[3 + a]) for a in range(3)], axis=0)
+
+        terms = pl.run_scoped(
+            weight_terms, *[pltpu.ACC(m)((128, 256), F32) for m in range(2) for _ in range(3)])
         for a in range(3):
             zero_side = pltpu.roll(terms[a * 128:a * 128 + 64], 64, 1)
             both_sides = zero_side + terms[a * 128 + 64:a * 128 + 128]

time: 66 us -> 60.4 us (0.915)
  Pallas kernels: 60.6 us -> 55 us
    pallas_call x1, Pallas kernels: 60.6 us -> 55 us  [all_grads(): pl.pallas_call(functools.partial(kernel, total, dps, secs), out_shape=(ja...]
where the time goes in v1:
time: 60.4 us; the launch traced here: 60 us
  Pallas kernels  55 us (91%)
  other arithmetic  3.5 us (6%)
  local copies, waits for them, and re-layouts  0.87 us (1%)
  between operations  0.68 us (1%)
    pallas_call x1, Pallas kernels, all_grads(): pl.pallas_call(functools.partial(kernel, total, dps, secs), out_shape=(ja...  55 us
    add x1, other arithmetic, per_device(): jnp.swapaxes(owned.reshape(blocks, convs, share, depth), 2, 3)  1.78 us

profile of v1, /device:TPU:0, one launch (start us, length us, event | category | flops | bytes accessed | tf_op | source)
XLA Modules:
  0.0 60.0 jit_solution(11069542651232123307)
XLA Ops:
  0.6 55.0 %shard_map.102 = (f32[6,16,576]{2,1,0:T(8,128)}, f32[32,128]{1,0:T(8,128)}) custom-call(bf16[64,4096]{1,0:T(8,128)(2,1)} %img_hbm.1, s32[1,64]{1,0:T(1,128)} %bitcast.20, f32[6,16,576]{2,1,0:T(8,128)} %bitcast.15, f32[3,2,64]{2,1,0:T(2,128)} %gain.1, f32[3,2,64]{2,1,0:T(2,128)} %bias.1, f32[10,64]{1,0:T(8,128)} %bitcast.17, f32[1,10]{1,0:T(1,128)} %bitcast.21), custom_call_target="tpu_custom_call" | custom-call | tf_op jit(solution)/shard_map/pallas_call | solution.py:402
  55.6 0.0 copy-start.2
  55.6 0.0 copy-start.3
  55.6 0.7 %slice.9 = f32[12,64]{1,0:T(8,128)S(1)} slice(f32[32,128]{1,0:T(8,128)} %get-tuple-element.7), slice={[0:12], [0:64]} | slice | bytes 6144 | tf_op jit(solution)/shard_map/slice | solution.py:453
  56.3 0.0 copy-start.1
  56.4 0.0 copy-done.2
  56.4 0.0 copy-done.3
  56.4 0.0 copy-start
  56.4 0.6 %fusion = f32[3,2,2,64]{3,2,1,0:T(2,128)} fusion(f32[3,2,2,64]{3,2,1,0:T(2,128)S(1)} %reshape.27, f32[3,2,1,64]{3,2,1,0:T(1,128)S(1)} %bitcast.19, f32[3,2,1,64]{3,2,1,0:T(1,128)S(1)} %bitcast.18), kind=kLoop, calls=%fused_computation.3 | loop fusion | flops 2304 | bytes 9216 | tf_op jit(solution)/shard_map/add | solution.py:453
  57.0 0.1 copy-done.1
  57.1 0.0 copy-done
  57.1 0.0 copy-start.4
  57.1 0.6 %bitcast_add_fusion = f32[64,10]{0,1:T(8,128)} fusion(f32[64,10]{0,1:T(8,128)S(1)} %copy-done, f32[32,128]{1,0:T(8,128)S(1)} %copy-done.1), kind=kLoop, calls=%fused_computation.1 | loop fusion | flops 1280 | bytes 7680 | tf_op jit(solution)/shard_map/add | solution.py:455
  57.7 0.1 copy-done.4
  57.7 0.5 bitcast_add_fusion.1
  58.2 1.8 %multiply_add_fusion = f32[3,2,576,16]{2,3,1,0:T(8,128)} fusion(f32[3,2,576,16]{2,3,1,0:T(8,128)} %bitcast.16, f32[3,2,576,16]{2,3,1,0:T(8,128)} %param.9), kind=kLoop, calls=%fused_computation | loop fusion | flops 110592 | bytes 663552 | tf_op jit(solution)/shard_map/add | solution.py:451
  (1 shorter events, 0.0 us)
Async XLA Ops:
  55.6 0.7 %copy-start.2 = (f32[3,2,64]{2,1,0:T(2,128)S(1)}, f32[3,2,64]{2,1,0:T(2,128)}, u32[]{:S(2)}) copy-start(f32[3,2,64]{2,1,0:T(2,128)} %gain.1) | copy-start | bytes 4612
  55.6 0.7 %copy-start.3 = (f32[3,2,64]{2,1,0:T(2,128)S(1)}, f32[3,2,64]{2,1,0:T(2,128)}, u32[]{:S(2)}) copy-start(f32[3,2,64]{2,1,0:T(2,128)} %bias.1) | copy-start | bytes 4612
  56.3 0.7 %copy-start.1 = (f32[32,128]{1,0:T(8,128)S(1)}, f32[32,128]{1,0:T(8,128)}, u32[]{:S(2)}) copy-start(f32[32,128]{1,0:T(8,128)} %get-tuple-element.7) | copy-start | bytes 49156
  56.4 0.7 %copy-start = (f32[64,10]{0,1:T(8,128)S(1)}, f32[64,10]{0,1:T(8,128)}, u32[]{:S(2)}) copy-start(f32[64,10]{0,1:T(8,128)} %param.12) | copy-start | bytes 7684
  57.1 0.7 %copy-start.4 = (f32[10]{0:T(128)S(1)}, f32[10]{0:T(128)}, u32[]{:S(2)}) copy-start(f32[10]{0:T(128)} %param.13) | copy-start | bytes 124

commit v2 on v1

--- a/solution.py
+++ b/solution.py
@@ -15,18 +15,25 @@
 OFFSETS = (0, 1, 2, -1)
 
 
-CHUNKS = ((5, 4), (3, 2), (1,), (0,))
-
-
-def chunk_tiles(c):
-    return 9 * len(CHUNKS[c]) + (3 if c == 0 else 1)
-
-
-def kernel(total, dps, secs, img_hbm, labels, own_hbm, gain, bias, hw, hb, conv_out, small,
+TILES = 5
+DIRECT = (1, 0)
+AFTER = {3: (("b", 5),), 2: (("b", 4),), 1: (("b", 3),)}
+TAIL = (("b", 2), ("c", 5), ("c", 4), ("b", 1), ("c", 3), ("b", 0), ("c", 2),
+        ("f", 5), ("f", 4), ("f", 3), ("f", 2), ("f", 1), ("f", 0))
+
+
+def owner(k, m, dps):
+    return (m * dps // TILES + 3 * k) % dps
+
+
+def kernel(total, dps, secs, img_hbm, labels, own_hbm, gain, bias, hw, hb,
+           conv_out, norm_out, hw_out, hb_out,
            xs, zs, dsw, rs, wf, wb, qs, qt, du2, du1, hw2, lab, wt, buf, in_a, tot, in_b,
            fin, img, own, load, w_send, w_recv, a_send, a_recv, b_send, b_recv, c_send, c_recv):
     dp, sec = lax.axis_index("dp"), lax.axis_index("section")
-    per = [-(-chunk_tiles(c) // dps) for c in range(len(CHUNKS))]
+    lane = lax.broadcasted_iota(jnp.int32, (1, 128), 1)
+    low = lane < 64
+    classes = hw.shape[0]
 
     load_own = pltpu.make_async_copy(own_hbm, own, load.at[0])
     load_img = pltpu.make_async_copy(img_hbm, img, load.at[1])
@@ -54,27 +61,36 @@
             recv_sem=w_recv.at[b, d - 1], device_id=(dp, lax.rem(sec + d, secs)),
             device_id_type=MESH)
 
-    def send_a(b, d):
+    def send_a(k, d):
         to = lax.rem(sec + d, secs)
         return pltpu.make_async_remote_copy(
-            src_ref=buf.at[b, to, pl.ds(0, chunk_tiles(b))],
-            dst_ref=in_a.at[b, d - 1, pl.ds(0, chunk_tiles(b))], send_sem=a_send.at[b, d - 1],
-            recv_sem=a_recv.at[b, d - 1], device_id=(dp, to), device_id_type=MESH)
-
-    def send_b(b, d):
+            src_ref=buf.at[k, to], dst_ref=in_a.at[k, sec], send_sem=a_send.at[k, d - 1],
+            recv_sem=a_recv.at[k, d - 1], device_id=(dp, to), device_id_type=MESH)
+
+    def send_tile(k, m):
+        to = owner(k, m, dps)
+        return pltpu.make_async_remote_copy(
+            src_ref=tot.at[k, m], dst_ref=in_b.at[k, dp, m], send_sem=b_send.at[k, m],
+            recv_sem=b_recv.at[k, lax.rem(to - dp + dps - 1, dps)],
+            device_id=(to, sec), device_id_type=MESH)
+
+    def wait_tile(k, m, d):
+        pltpu.make_async_remote_copy(
+            src_ref=tot.at[k, m], dst_ref=in_b.at[k, lax.rem(dp - d + dps, dps), m],
+            send_sem=b_send.at[k, m], recv_sem=b_recv.at[k, d - 1],
+            device_id=(lax.rem(dp + d, dps), sec), device_id_type=MESH).wait_recv()
+
+    def send_all(k, d):
         to = lax.rem(dp + d, dps)
         return pltpu.make_async_remote_copy(
-            src_ref=tot.at[b, pl.ds(to * per[b], per[b])],
-            dst_ref=in_b.at[b, d - 1, pl.ds(0, per[b])],
-            send_sem=b_send.at[b, d - 1], recv_sem=b_recv.at[b, d - 1],
-            device_id=(to, sec), device_id_type=MESH)
-
-    def send_c(b, d):
-        to = lax.rem(dp + d, dps)
-        mine = fin.at[b, pl.ds(dp * per[b], per[b])]
+            src_ref=tot.at[k], dst_ref=in_b.at[k, dp], send_sem=b_send.at[k, d - 1],
+            recv_sem=b_recv.at[k, d - 1], device_id=(to, sec), device_id_type=MESH)
+
+    def send_c(k, m, d):
         return pltpu.make_async_remote_copy(
-            src_ref=mine, dst_ref=mine, send_sem=c_send.at[b, d - 1],
-            recv_sem=c_recv.at[b, d - 1], device_id=(to, sec), device_id_type=MESH)
+            src_ref=fin.at[k, m], dst_ref=fin.at[k, m], send_sem=c_send.at[k, d - 1],
+            recv_sem=c_recv.at[k, m], device_id=(lax.rem(dp + d, dps), sec),
+            device_id_type=MESH)
 
     def each_dp(act):
         def step(d, carry):
@@ -82,37 +98,79 @@
             return carry
         lax.fori_loop(1, dps, step, 0)
 
-    def start_a(b):
+    def resplit(v):
+        whole = v[0:8] + v[8:16]
+        top = whole.astype(BF16).astype(F32)
+        return jnp.where(low, v, jnp.concatenate([top, whole - top], axis=0))
+
+    def start_a(k):
         for d in range(1, secs):
-            send_a(b, d).start()
-
-    def start_b(b):
+            send_a(k, d).start()
+        in_a[k, sec] = buf[k, sec]
+
+    def start_b(k):
         for d in range(1, secs):
-            send_a(b, d).wait_recv()
-        tiles = chunk_tiles(b)
-        all_terms = buf[b, sec, 0:tiles]
-        for d in range(1, secs):
-            all_terms = all_terms + in_a[b, d - 1, 0:tiles]
-        tot[b, 0:tiles] = all_terms
-        if tot.shape[1] > tiles:
-            tot[b, tiles:] = jnp.zeros((tot.shape[1] - tiles, 8, 128), F32)
-        each_dp(lambda d: send_b(b, d).start())
-
-    def start_c(b):
-        each_dp(lambda d: send_b(b, d).wait_recv())
-        sums = lax.fori_loop(1, dps, lambda d, acc: acc + in_b[b, d - 1, 0:per[b]],
-                             tot[b, pl.ds(dp * per[b], per[b])])
-        fin[b, pl.ds(dp * per[b], per[b])] = sums
-        each_dp(lambda d: send_c(b, d).start())
-
-    def end_c(b):
-        each_dp(lambda d: send_c(b, d).wait_recv())
+            send_a(k, d).wait_recv()
+        for m in range(TILES):
+            v = in_a[k, 0, m].astype(F32)
+            for q in range(1, secs):
+                v = v + in_a[k, q, m].astype(F32)
+            tot[k, m] = (resplit(v) if m == TILES - 1 else v).astype(BF16)
+        if k in DIRECT:
+            each_dp(lambda d: send_all(k, d).start())
+            in_b[k, dp] = tot[k]
+            return
+        for m in range(TILES):
+            @pl.when(dp != owner(k, m, dps))
+            def _():
+                send_tile(k, m).start()
+
+            @pl.when(dp == owner(k, m, dps))
+            def _():
+                in_b[k, dp, m] = tot[k, m]
+
+    def sum_b(k, m):
+        v = lax.fori_loop(1, dps, lambda p, acc: acc + in_b[k, p, m].astype(F32),
+                          in_b[k, 0, m].astype(F32))
+        fin[k, m] = (resplit(v) if m == TILES - 1 else v).astype(BF16)
+
+    def start_c(k):
+        for m in range(TILES):
+            @pl.when(dp == owner(k, m, dps))
+            def _():
+                each_dp(lambda d: wait_tile(k, m, d))
+                sum_b(k, m)
+                each_dp(lambda d: send_c(k, m, d).start())
+
+    def finish(k):
+        if k in DIRECT:
+            each_dp(lambda d: pltpu.make_async_remote_copy(
+                src_ref=tot.at[k], dst_ref=in_b.at[k, lax.rem(dp - d + dps, dps)],
+                send_sem=b_send.at[k, d - 1], recv_sem=b_recv.at[k, d - 1],
+                device_id=(lax.rem(dp + d, dps), sec), device_id_type=MESH).wait_recv())
+            for m in range(TILES):
+                sum_b(k, m)
+        else:
+            for m in range(TILES):
+                @pl.when(dp != owner(k, m, dps))
+                def _():
+                    send_c(k, m, 1).wait_recv()
+        rows = [fin[k, m].astype(F32) for m in range(TILES)]
+        side = pltpu.roll(rows[-1][0:8] + rows[-1][8:16], 64, 1)[:, 0:64]
+        conv_out[k] = (jnp.concatenate(rows[:-1] + [rows[-1][:, 0:64]], axis=1)
+                       + prior_precision * own[k])
+        b, j = k // 2, k % 2
+        norm_out[b, j, 0:1] = side[0:1] + prior_precision * gain[b, j:j + 1, :]
+        norm_out[b, j, 1:2] = side[1:2] + prior_precision * bias[b, j:j + 1, :]
+        if k == 5:
+            hw_out[0:6] = side[2:8] + prior_precision * hw[0:6]
+        if k == 4:
+            hw_out[6:classes] = side[2:classes - 4] + prior_precision * hw[6:classes]
+            hb_out[...] = side[6:7, 0:classes] + prior_precision * hb[...]
 
     for b in range(3):
         for d in range(1, secs):
             send_w(b, d).start()
-    lane = lax.broadcasted_iota(jnp.int32, (1, 128), 1)
-    low = lane < 64
 
     def both(v):
         return v + pltpu.roll(v, 64, 1)
@@ -257,7 +315,6 @@
     hw2[0:hw.shape[0], :] = twice(hw[...])
     lab[...] = jnp.zeros((8, 128), jnp.int32)
     lab[0:1, 0:64] = labels[...]
-    classes = hw.shape[0]
     hbias = jnp.concatenate([hb[...], jnp.zeros((1, 128 - classes), F32)], axis=1)
     logits = dot_f32(jnp.where(low, pooled, 0.0), hw2[...].T) + hbias
     live = lane < classes
@@ -272,12 +329,19 @@
     tall = jnp.concatenate([pooled, jnp.zeros((64, 128), F32)], axis=0)
     d_head = dot_f32(dlt[0:16], tall)
     row = lax.broadcasted_iota(jnp.int32, (8, 128), 0)
-    extra = jnp.where(row == 4, jnp.sum(dl, axis=0, keepdims=True), 0.0)
-    for q in range(secs):
-        buf[0, q, 19] = d_head[0:8]
-        buf[0, q, 20] = d_head[8:16]
+    d_bias = pltpu.roll(jnp.sum(dl, axis=0, keepdims=True), 64, 1)
+    head_rows = {
+        5: jnp.where(row >= 2, pltpu.roll(d_head[0:8], 2, 0), 0.0),
+        4: jnp.where(row == 6, d_bias,
+                     jnp.where(row >= 4, pltpu.roll(d_head[8:16], 4, 0),
+                               pltpu.roll(d_head[0:8], 4, 0))),
+    }
     spread_g = dot_f32(dl, hw2[...]) * (1.0 / 64)
     spread_g = spread_g.astype(BF16).astype(F32)
+
+    def advance(k):
+        for act, other in AFTER.get(k, ()):
+            {"b": start_b, "c": start_c}[act](other)
 
     def tally(k, y, d, sums):
         return (sums[0] + over_pairs(d * zs[k, y]), sums[1] + over_pairs(d))
@@ -291,18 +355,14 @@
     for k in range(5, -1, -1):
         b, j = k // 2, k % 2
         source = du2 if j == 1 else du1
-        c = [k in ks for ks in CHUNKS].index(True)
-        at_tile = CHUNKS[c].index(k)
-        ends = k == CHUNKS[c][-1]
         r = rs[k]
         dg = both(sums[0]) * r
         db = both(sums[1])
-        extra = jnp.where(row == 2 * at_tile, jnp.sum(dg, axis=0, keepdims=True), extra)
-        extra = jnp.where(row == 2 * at_tile + 1, jnp.sum(db, axis=0, keepdims=True), extra)
-        if ends:
-            for q in range(secs):
-                buf[c, q, 9 * len(CHUNKS[c])] = extra
-            extra = jnp.zeros((8, 128), F32)
+        extra = jnp.where(row == 0, jnp.sum(dg, axis=0, keepdims=True),
+                          jnp.where(row == 1, jnp.sum(db, axis=0, keepdims=True),
+                                    head_rows.get(k, 0.0)))
+        top = extra.astype(BF16).astype(F32)
+        side = jnp.concatenate([top, extra - top] * secs, axis=0)
         c1 = r * twice(gain[b, j:j + 1, :])
         c2 = c1 * dg * r * (1.0 / 64)
 
@@ -329,24 +389,20 @@
 
         terms = pl.run_scoped(
             weight_terms, *[pltpu.ACC(m)((128, 256), F32) for m in range(2) for _ in range(3)])
-        for a in range(3):
-            zero_side = pltpu.roll(terms[a * 128:a * 128 + 64], 64, 1)
-            both_sides = zero_side + terms[a * 128 + 64:a * 128 + 128]
-            for e in range(3):
-                at = e // 2 * 128
-                here = both_sides[:, at:at + 128]
-                there = pltpu.roll(here, 64, 1)
-                first, second = (here, there) if e % 2 == 0 else (there, here)
-                for q in range(secs):
-                    buf[c, q, at_tile * 9 + a * 3 + e] = jnp.where(
-                        low, first[q * 16:q * 16 + 8], second[q * 16 + 8:q * 16 + 16])
-
-        if ends:
-            start_a(c)
-        if k == 3:
-            start_b(0)
-        if k == 2:
-            start_c(0)
+        def rolled(a):
+            return (pltpu.roll(terms[a * 128:a * 128 + 64], 64, 1)
+                    + terms[a * 128 + 64:a * 128 + 128])
+
+        first, last = rolled(0), rolled(2)
+        swapped = jnp.concatenate([terms[128:192, 128:256], terms[128:192, 0:128]], axis=1)
+        middle = swapped + pltpu.roll(terms[192:256], 64, 1)
+        tiles = [first[:, 0:128], jnp.where(low, first[:, 128:256], middle[:, 0:128]),
+                 middle[:, 128:256], last[:, 0:128], jnp.where(low, last[:, 128:256], side)]
+        for m in range(TILES):
+            v = tiles[m].astype(BF16)
+            for q in range(secs):
+                buf[k, q, m] = v[q * 16:q * 16 + 16]
+        start_a(k)
 
         if j == 1:
             def to_first(y, out, sums):
@@ -355,8 +411,7 @@
                 return tally(k - 1, y, d, sums)
 
             sums = conv(qs, wb.at[k], to_first, (zero_sum, zero_sum))
-            if k == 1:
-                start_b(1)
+            advance(k)
         elif k > 0:
             def to_second(y, out, sums):
                 g = (du2[y] + out).astype(BF16).astype(F32)
@@ -365,46 +420,41 @@
                 return tally(k - 1, y, d, sums)
 
             sums = conv(qs, wb.at[k], to_second, (zero_sum, zero_sum))
-
-    start_c(1)
-    start_b(2)
-    start_b(3)
-    start_c(2)
-    start_c(3)
-    for c, ks in enumerate(CHUNKS):
-        end_c(c)
-        for at_tile, k in enumerate(ks):
-            rows = [fin[c, at_tile * 9 + t] for t in range(9)]
-            conv_out[k, 0:8] = jnp.concatenate([v[:, 0:64] for v in rows], axis=1)
-            conv_out[k, 8:16] = jnp.concatenate([v[:, 64:128] for v in rows], axis=1)
-            small[2 * k:2 * k + 2] = fin[c, 9 * len(ks)][2 * at_tile:2 * at_tile + 2]
-        if c == 0:
-            small[12:13] = fin[c, 18][4:5]
-            small[16:24] = fin[c, 19]
-            small[24:32] = fin[c, 20]
+            advance(k)
+
+    for act, k in TAIL:
+        {"b": start_b, "c": start_c, "f": finish}[act](k)
     for b in range(3):
         for d in range(1, secs):
             send_w(b, d).wait_send()
-    for c in range(len(CHUNKS)):
+    for k in range(6):
         for d in range(1, secs):
-            send_a(c, d).wait_send()
-        each_dp(lambda d: send_b(c, d).wait_send())
-        each_dp(lambda d: send_c(c, d).wait_send())
+            send_a(k, d).wait_send()
+        if k in DIRECT:
+            each_dp(lambda d: send_all(k, d).wait_send())
+            continue
+        for m in range(TILES):
+            @pl.when(dp != owner(k, m, dps))
+            def _():
+                send_tile(k, m).wait_send()
+
+            @pl.when(dp == owner(k, m, dps))
+            def _():
+                each_dp(lambda d: send_c(k, m, d).wait_send())
 
 
 def all_grads(total, dps, secs, images_in, labels, own, gain, bias, hw, hb):
     vmem = pl.BlockSpec(memory_space=pltpu.VMEM)
-    chunks = len(CHUNKS)
-    tiles = max(chunk_tiles(c) for c in range(chunks))
-    per = -(-tiles // dps)
     hbm = pl.BlockSpec(memory_space=pltpu.HBM)
     dma = pltpu.SemaphoreType.DMA
     return pl.pallas_call(
         functools.partial(kernel, total, dps, secs),
         out_shape=(jax.ShapeDtypeStruct(own.shape, F32),
-                   jax.ShapeDtypeStruct((32, 128), F32)),
+                   jax.ShapeDtypeStruct(gain.shape[:2] + (2,) + gain.shape[2:], F32),
+                   jax.ShapeDtypeStruct(hw.shape, F32),
+                   jax.ShapeDtypeStruct(hb.shape, F32)),
         in_specs=[hbm, vmem, hbm, vmem, vmem, vmem, vmem],
-        out_specs=(vmem, vmem),
+        out_specs=(vmem, vmem, vmem, vmem),
         scratch_shapes=[
             pltpu.VMEM((6, 10, 256, 256), BF16),
             pltpu.VMEM((6, 8, 256, 128), F32),
@@ -419,18 +469,18 @@
             pltpu.VMEM((128, 128), F32),
             pltpu.VMEM((8, 128), jnp.int32),
             pltpu.VMEM((secs,) + own.shape, BF16),
-            pltpu.VMEM((chunks, secs, tiles, 8, 128), F32),
-            pltpu.VMEM((chunks, secs - 1, tiles, 8, 128), F32),
-            pltpu.VMEM((chunks, per * dps, 8, 128), F32),
-            pltpu.VMEM((chunks, dps - 1, per, 8, 128), F32),
-            pltpu.VMEM((chunks, per * dps, 8, 128), F32),
+            pltpu.VMEM((6, secs, TILES, 16, 128), BF16),
+            pltpu.VMEM((6, secs, TILES, 16, 128), BF16),
+            pltpu.VMEM((6, TILES, 16, 128), BF16),
+            pltpu.VMEM((6, dps, TILES, 16, 128), BF16),
+            pltpu.VMEM((6, TILES, 16, 128), BF16),
             pltpu.VMEM(images_in.shape, BF16),
             pltpu.VMEM(own.shape, F32),
             dma((2,)),
             dma((3, secs - 1)), dma((3, secs - 1)),
-            dma((chunks, secs - 1)), dma((chunks, secs - 1)),
-            dma((chunks, dps - 1)), dma((chunks, dps - 1)),
-            dma((chunks, dps - 1)), dma((chunks, dps - 1)),
+            dma((6, secs - 1)), dma((6, secs - 1)),
+            dma((6, max(dps - 1, TILES))), dma((6, dps)),
+            dma((6, dps)), dma((6, TILES)),
         ],
         compiler_params=pltpu.CompilerParams(
             vmem_limit_bytes=63 * 1024 * 1024 + 768 * 1024, collective_id=0, has_side_effects=True),
@@ -442,19 +492,11 @@
     dps, secs = lax.axis_size("dp"), lax.axis_size("section")
     blocks, convs, depth, share = conv_weight.shape
     own = jnp.swapaxes(conv_weight, 2, 3).reshape(blocks * convs, share, depth)
-    owned, small = all_grads(images * dps * secs, dps, secs, images_in,
-                             labels.reshape(1, images), own, frn_gain,
-                             frn_bias, head_weight.T, head_bias.reshape(1, -1))
-    classes = head_bias.shape[0]
-    params = jnp.stack([frn_gain, frn_bias], axis=2)
-    return (
-        jnp.swapaxes(owned.reshape(blocks, convs, share, depth), 2, 3)
-        + prior_precision * conv_weight,
-        small[0:12, 0:64].reshape(params.shape)
-        + prior_precision * params,
-        small[16:16 + classes, 0:64].T + prior_precision * head_weight,
-        small[12, 0:classes] + prior_precision * head_bias,
-    )
+    conv, norm, head, head_b = all_grads(
+        images * dps * secs, dps, secs, images_in, labels.reshape(1, images), own, frn_gain,
+        frn_bias, head_weight.T, head_bias.reshape(1, -1))
+    return (jnp.swapaxes(conv.reshape(blocks, convs, share, depth), 2, 3), norm, head.T,
+            head_b.reshape(-1))
 
 
 def solution(mesh):

time: 60.4 us -> 51.9 us (0.86)
  Pallas kernels: 55 us -> 47.6 us
  other arithmetic: 3.5 us -> 0 us
  local copies, waits for them, and re-layouts: 0.87 us -> 3.48 us
    pallas_call x1, Pallas kernels: 55 us -> 47.6 us  [all_grads(): pl.pallas_call(functools.partial(kernel, total, dps, secs), out_shape=(ja...]
    add x4 -> x0, other arithmetic: 3.5 us -> none  [the longest x1 1.78 us: per_device(): jnp.swapaxes(owned.reshape(blocks, convs, share, depth), 2, 3)]
    unnamed x10, local copies, waits for them, and re-layouts: 0.16 us -> 3.48 us
    slice x1 -> x0, local copies, waits for them, and re-layouts: 0.71 us -> none  [per_device(): small[0:12, 0:64].reshape(params.shape) + prior_precision * params]
where the time goes in v2:
time: 51.9 us; the launch traced here: 51.7 us
  Pallas kernels  47.6 us (92%)
  local copies, waits for them, and re-layouts  3.48 us (7%)
  between operations  0.65 us (1%)
    pallas_call x1, Pallas kernels, all_grads(): pl.pallas_call(functools.partial(kernel, total, dps, secs), out_shape=(ja...  47.6 us
    unnamed x10, local copies, waits for them, and re-layouts  3.48 us

profile of v2, /device:TPU:0, one launch (start us, length us, event | category | flops | bytes accessed | tf_op | source)
XLA Modules:
  0.0 51.7 jit_solution(867352636582172519)
XLA Ops:
  0.6 47.6 %shard_map.102 = (f32[6,16,576]{2,1,0:T(8,128)}, f32[3,2,2,64]{3,2,1,0:T(2,128)}, f32[10,64]{1,0:T(8,128)}, f32[1,10]{1,0:T(1,128)}) custom-call(bf16[64,4096]{1,0:T(8,128)(2,1)} %img_hbm.1, s32[1,64]{1,0:T(1,128)} %bitcast.15, f32[6,16,576]{2,1,0:T(8,128)} %bitcast.11, f32[3,2,64]{2,1,0:T(2,128)} %gain.1, f32[3,2,64]{2,1,0:T(2,128)} %bias.1, ...), custom_call_target="tpu_custom_call" | custom-call | tf_op jit(solution)/shard_map/pallas_call | solution.py:450
  48.2 0.0 copy-start.1
  48.2 1.7 %copy.15 = f32[3,2,576,16]{2,3,1,0:T(8,128)} copy(f32[3,2,576,16]{2,3,1,0:T(8,128)} %bitcast.12) | data formatting | bytes 442368
  49.9 0.0 copy-done.1
  49.9 0.0 copy-start
  49.9 0.6 %copy.16 = f32[3,2,2,64]{3,2,1,0:T(2,128)} copy(f32[3,2,2,64]{3,2,1,0:T(2,128)S(1)} %copy-done.1) | data formatting | bytes 6144
  50.5 0.1 copy-done
  50.6 0.0 copy-start.2
  50.6 0.6 %copy.17 = f32[64,10]{0,1:T(8,128)} copy(f32[64,10]{0,1:T(8,128)S(1)} %bitcast.14) | data formatting | bytes 5120
  51.2 0.0 copy-done.2
  51.2 0.5 copy.18
Async XLA Ops:
  48.2 1.7 %copy-start.1 = (f32[3,2,2,64]{3,2,1,0:T(2,128)S(1)}, f32[3,2,2,64]{3,2,1,0:T(2,128)}, u32[]{:S(2)}) copy-start(f32[3,2,2,64]{3,2,1,0:T(2,128)} %get-tuple-element.17) | copy-start | bytes 9220
  49.9 0.7 %copy-start = (f32[10,64]{1,0:T(8,128)S(1)}, f32[10,64]{1,0:T(8,128)}, u32[]{:S(2)}) copy-start(f32[10,64]{1,0:T(8,128)} %get-tuple-element.10) | copy-start | bytes 7684
  50.6 0.6 %copy-start.2 = (f32[1,10]{1,0:T(1,128)S(1)}, f32[1,10]{1,0:T(1,128)}, u32[]{:S(2)}) copy-start(f32[1,10]{1,0:T(1,128)} %get-tuple-element.11) | copy-start | bytes 124

commit v3 on v2

--- a/solution.py
+++ b/solution.py
@@ -54,11 +54,11 @@
     wt[sec] = own[...].astype(BF16)
     pl.semaphore_wait(barrier, secs - 1 + dps - 1)
 
-    def send_w(b, d):
-        mine = wt.at[sec, pl.ds(2 * b, 2)]
+    def send_w(k, d):
+        mine = wt.at[sec, k]
         return pltpu.make_async_remote_copy(
-            src_ref=mine, dst_ref=mine, send_sem=w_send.at[b, d - 1],
-            recv_sem=w_recv.at[b, d - 1], device_id=(dp, lax.rem(sec + d, secs)),
+            src_ref=mine, dst_ref=mine, send_sem=w_send.at[k, d - 1],
+            recv_sem=w_recv.at[k, d - 1], device_id=(dp, lax.rem(sec + d, secs)),
             device_id_type=MESH)
 
     def send_a(k, d):
@@ -168,9 +168,9 @@
             hw_out[6:classes] = side[2:classes - 4] + prior_precision * hw[6:classes]
             hb_out[...] = side[6:7, 0:classes] + prior_precision * hb[...]
 
-    for b in range(3):
+    for k in range(6):
         for d in range(1, secs):
-            send_w(b, d).start()
+            send_w(k, d).start()
 
     def both(v):
         return v + pltpu.roll(v, 64, 1)
@@ -238,53 +238,43 @@
                           for j in range(4)], axis=0).astype(F32)
         put(xs.at[0], y, slab)
 
-    def spread(b):
+    def spread(k):
+        b, j = k // 2, k % 2
         for d in range(1, secs):
-            send_w(b, d).wait_recv()
-        flat = jnp.concatenate(
-            [wt[q, 2 * b + j] for j in range(2) for q in range(secs)], axis=0).astype(F32)
+            send_w(k, d).wait_recv()
         zero = jnp.zeros((64, 128), BF16)
-        cols = jnp.concatenate([flat, jnp.zeros((128, 64), F32)], axis=1).T
+        none = jnp.zeros((64, 128), F32)
+        flat = jnp.concatenate([wt[q, k] for q in range(secs)], axis=0).astype(F32)
+        wide = jnp.concatenate([none[:, 0:64], flat, none], axis=1)
+        square = jnp.concatenate([flat, none[:, 0:64]], axis=1)
+        cols = jnp.concatenate([square, square], axis=0).T
         plain = [cols[t * 64:(t + 1) * 64] for t in range(9)]
-        turned = [pltpu.roll(v, 64, 1) for v in plain]
-        none = jnp.zeros((64, 128), F32)
-        for j in range(2):
-            first, second = (plain, turned) if j == 0 else (turned, plain)
-            for a in range(3):
-                for s, xi in enumerate(OFFSETS):
-                    left = first[a * 3 + xi + 1] if 0 <= xi + 1 <= 2 else none
-                    right = second[a * 3 + xi] if 0 <= xi <= 2 else none
-                    tile = jnp.where(low, left, right).astype(BF16)
-                    for yo in range(2):
-                        row = (a + yo) * 256 + s * 64
-                        wf[2 * b + j, row:row + 64, yo * 128:yo * 128 + 128] = tile
-        wide = jnp.concatenate(
-            [jnp.zeros((128, 64), F32), flat, jnp.zeros((128, 128), F32)], axis=1)
         for a in range(3):
             for s, xi in enumerate(OFFSETS):
+                left = plain[a * 3 + xi + 1] if 0 <= xi + 1 <= 2 else none
+                right = plain[a * 3 + xi] if 0 <= xi <= 2 else none
+                tile = jnp.where(low, left, right).astype(BF16)
                 at = ((2 - a) * 3 + 2 - xi) * 64
-                tile = wide[:, at:at + 128]
+                back = wide[:, at:at + 128]
                 if xi == -1:
-                    tile = jnp.where(low, tile, 0.0)
+                    back = jnp.where(low, back, 0.0)
                 if xi == 2:
-                    tile = jnp.where(low, 0.0, tile)
-                tile = tile.astype(BF16)
-                for j in range(2):
-                    for yo in range(2):
-                        row = (a + yo) * 256 + s * 64
-                        wb[2 * b + j, row:row + 64, yo * 128:yo * 128 + 128] = (
-                            tile[j * 64:j * 64 + 64])
-        for j in range(2):
-            for ref in (wf, wb):
-                for s in range(4):
-                    ref[2 * b + j, 768 + s * 64:832 + s * 64, 0:128] = zero
-                    ref[2 * b + j, s * 64:s * 64 + 64, 128:256] = zero
+                    back = jnp.where(low, 0.0, back)
+                back = back.astype(BF16)
+                for yo in range(2):
+                    row = (a + yo) * 256 + s * 64
+                    wf[k, row:row + 64, yo * 128:yo * 128 + 128] = tile
+                    if k > 0:
+                        wb[k, row:row + 64, yo * 128:yo * 128 + 128] = back
+        for ref in (wf, wb):
+            for s in range(4):
+                ref[k, 768 + s * 64:832 + s * 64, 0:128] = zero
+                ref[k, s * 64:s * 64 + 64, 128:256] = zero
 
     pooled = zero_sum
     for k in range(6):
         b, j = k // 2, k % 2
-        if j == 0:
-            spread(b)
+        spread(k)
 
         def keep(y, out, energy):
             zs[k, y] = out
@@ -374,7 +364,7 @@
             qt[y + 1] = d.reshape(256, 128).T.astype(BF16)
             return carry
 
-        lax.fori_loop(0, 8, settle, 0)
+        lax.fori_loop(0, 8, settle, 0, unroll=8)
 
         def weight_terms(*accs):
             for step in range(4):
@@ -424,9 +414,9 @@
 
     for act, k in TAIL:
         {"b": start_b, "c": start_c, "f": finish}[act](k)
-    for b in range(3):
+    for k in range(6):
         for d in range(1, secs):
-            send_w(b, d).wait_send()
+            send_w(k, d).wait_send()
     for k in range(6):
         for d in range(1, secs):
             send_a(k, d).wait_send()
@@ -477,7 +467,7 @@
             pltpu.VMEM(images_in.shape, BF16),
             pltpu.VMEM(own.shape, F32),
             dma((2,)),
-            dma((3, secs - 1)), dma((3, secs - 1)),
+            dma((6, secs - 1)), dma((6, secs - 1)),
             dma((6, secs - 1)), dma((6, secs - 1)),
             dma((6, max(dps - 1, TILES))), dma((6, dps)),
             dma((6, dps)), dma((6, TILES)),
@@ -487,14 +477,30 @@
     )(images_in, labels, own, gain, bias, hw, hb)
 
 
+def hand_over(*refs):
+    half = len(refs) // 2
+    for i in range(half):
+        refs[half + i][...] = refs[i][...]
+
+
+def outputs(*arrays):
+    vmem = pl.BlockSpec(memory_space=pltpu.VMEM)
+    return pl.pallas_call(
+        hand_over,
+        out_shape=tuple(jax.ShapeDtypeStruct(v.shape, v.dtype) for v in arrays),
+        in_specs=[vmem] * len(arrays),
+        out_specs=(vmem,) * len(arrays),
+    )(*arrays)
+
+
 def per_device(images_in, labels, conv_weight, frn_gain, frn_bias, head_weight, head_bias):
     images = images_in.shape[0]
     dps, secs = lax.axis_size("dp"), lax.axis_size("section")
     blocks, convs, depth, share = conv_weight.shape
     own = jnp.swapaxes(conv_weight, 2, 3).reshape(blocks * convs, share, depth)
-    conv, norm, head, head_b = all_grads(
+    conv, norm, head, head_b = outputs(*all_grads(
         images * dps * secs, dps, secs, images_in, labels.reshape(1, images), own, frn_gain,
-        frn_bias, head_weight.T, head_bias.reshape(1, -1))
+        frn_bias, head_weight.T, head_bias.reshape(1, -1)))
     return (jnp.swapaxes(conv.reshape(blocks, convs, share, depth), 2, 3), norm, head.T,
             head_b.reshape(-1))
 

time: 51.9 us -> 46.9 us (0.904)
  local copies, waits for them, and re-layouts: 3.48 us -> 0 us
  Pallas kernels: 47.6 us -> 46 us
    unnamed x10 -> x0, local copies, waits for them, and re-layouts: 3.48 us -> none
    pallas_call x1, Pallas kernels: 47.6 us -> 44.3 us  [all_grads(): pl.pallas_call(functools.partial(kernel, total, dps, secs), out_shape=(ja...]
    pallas_call x0 -> x1, Pallas kernels: none -> 1.68 us  [outputs(): pl.pallas_call(hand_over, out_shape=tuple((jax.ShapeDtypeStruct(v.shape,...]
where the time goes in v3:
time: 46.9 us; the launch traced here: 46.7 us
  Pallas kernels  46 us (98%)
  between operations  0.64 us (1%)
    pallas_call x1, Pallas kernels, all_grads(): pl.pallas_call(functools.partial(kernel, total, dps, secs), out_shape=(ja...  44.3 us
    pallas_call x1, Pallas kernels, outputs(): pl.pallas_call(hand_over, out_shape=tuple((jax.ShapeDtypeStruct(v.shape,...  1.68 us

profile of v3, /device:TPU:0, one launch (start us, length us, event | category | flops | bytes accessed | tf_op | source)
XLA Modules:
  0.0 46.7 jit_solution(7308515224716314749)
XLA Ops:
  0.6 44.3 %shard_map.102 = (f32[6,16,576]{2,1,0:T(8,128)}, f32[3,2,2,64]{3,2,1,0:T(2,128)}, f32[10,64]{1,0:T(8,128)}, f32[1,10]{1,0:T(1,128)}) custom-call(bf16[64,4096]{1,0:T(8,128)(2,1)} %img_hbm.1, s32[1,64]{1,0:T(1,128)} %bitcast.13, f32[6,16,576]{2,1,0:T(8,128)} %bitcast.11, f32[3,2,64]{2,1,0:T(2,128)} %gain.1, f32[3,2,64]{2,1,0:T(2,128)} %bias.1, ...), custom_call_target="tpu_custom_call" | custom-call | tf_op jit(solution)/shard_map/pallas_call | solution.py:440
  45.0 1.7 %shard_map.103 = (f32[6,16,576]{2,1,0:T(8,128)}, f32[3,2,2,64]{3,2,1,0:T(2,128)}, f32[10,64]{1,0:T(8,128)}, f32[1,10]{1,0:T(1,128)}) custom-call(f32[6,16,576]{2,1,0:T(8,128)} %get-tuple-element.12.refs_0_, f32[3,2,2,64]{3,2,1,0:T(2,128)} %get-tuple-element.13.refs_1_, f32[10,64]{1,0:T(8,128)} %get-tuple-element.14.refs_2_, f32[1,10]{1,0:T(1,128)} %get-tuple-element.15.refs_3_), custom_call_target="tpu_custom_call" | custom-call | tf_op jit(solution)/shard_map/pallas_call | solution.py:488

commit v4 on v3

--- a/solution.py
+++ b/solution.py
@@ -16,43 +16,45 @@
 
 
 TILES = 5
-DIRECT = (1, 0)
-AFTER = {3: (("b", 5),), 2: (("b", 4),), 1: (("b", 3),)}
-TAIL = (("b", 2), ("c", 5), ("c", 4), ("b", 1), ("c", 3), ("b", 0), ("c", 2),
-        ("f", 5), ("f", 4), ("f", 3), ("f", 2), ("f", 1), ("f", 0))
-
-
-def owner(k, m, dps):
-    return (m * dps // TILES + 3 * k) % dps
+AFTER = {1: (("b", 5),)}
+TAIL = (("b", 4), ("b", 3), ("b", 2), ("b", 1), ("f", 5), ("b", 0), ("f", 4), ("f", 3),
+        ("f", 2), ("f", 1), ("f", 0))
 
 
 def kernel(total, dps, secs, img_hbm, labels, own_hbm, gain, bias, hw, hb,
            conv_out, norm_out, hw_out, hb_out,
-           xs, zs, dsw, rs, wf, wb, qs, qt, du2, du1, hw2, lab, wt, buf, in_a, tot, in_b,
-           fin, img, own, load, w_send, w_recv, a_send, a_recv, b_send, b_recv, c_send, c_recv):
+           xs, zs, dsw, rs, wf, wb, qs, qt, du2, du1, hw2, lab, wt, buf, in_a, in_b, img, own, load, w_send, w_recv, a_send, a_recv, b_send, b_recv):
     dp, sec = lax.axis_index("dp"), lax.axis_index("section")
     lane = lax.broadcasted_iota(jnp.int32, (1, 128), 1)
     low = lane < 64
     classes = hw.shape[0]
+    pair = 2 if dps % 2 == 0 else 1
+    group, rows_of = pair * secs, dps // pair
+    line, side_of = dp // pair, lax.rem(dp, pair)
+    mine = side_of * secs + sec
+
+    def each(n, act):
+        def step(d, carry):
+            act(d)
+            return carry
+        lax.fori_loop(1, n, step, 0)
 
     load_own = pltpu.make_async_copy(own_hbm, own, load.at[0])
     load_img = pltpu.make_async_copy(img_hbm, img, load.at[1])
     load_own.start()
     load_img.start()
     barrier = pltpu.get_barrier_semaphore()
-    for d in range(1, secs):
-        pl.semaphore_signal(barrier, inc=1, device_id=(dp, lax.rem(sec + d, secs)),
+    for d in range(1, group):
+        to = lax.rem(mine + d, group)
+        pl.semaphore_signal(barrier, inc=1,
+                            device_id=(line * pair + to // secs, lax.rem(to, secs)),
                             device_id_type=MESH)
-
-    def greet(d, carry):
-        pl.semaphore_signal(barrier, inc=1, device_id=(lax.rem(dp + d, dps), sec),
-                            device_id_type=MESH)
-        return carry
-
-    lax.fori_loop(1, dps, greet, 0)
+    each(rows_of, lambda d: pl.semaphore_signal(
+        barrier, inc=1, device_id=(lax.rem(line + d, rows_of) * pair + side_of, sec),
+        device_id_type=MESH))
     load_own.wait()
     wt[sec] = own[...].astype(BF16)
-    pl.semaphore_wait(barrier, secs - 1 + dps - 1)
+    pl.semaphore_wait(barrier, group - 1 + rows_of - 1)
 
     def send_w(k, d):
         mine = wt.at[sec, k]
@@ -62,41 +64,26 @@
             device_id_type=MESH)
 
     def send_a(k, d):
-        to = lax.rem(sec + d, secs)
+        to = lax.rem(mine + d, group)
         return pltpu.make_async_remote_copy(
-            src_ref=buf.at[k, to], dst_ref=in_a.at[k, sec], send_sem=a_send.at[k, d - 1],
-            recv_sem=a_recv.at[k, d - 1], device_id=(dp, to), device_id_type=MESH)
-
-    def send_tile(k, m):
-        to = owner(k, m, dps)
+            src_ref=buf.at[k, lax.rem(to, secs)], dst_ref=in_a.at[k, mine],
+            send_sem=a_send.at[k, d - 1], recv_sem=a_recv.at[k, d - 1],
+            device_id=(line * pair + to // secs, lax.rem(to, secs)), device_id_type=MESH)
+
+    def wait_a(k, d):
+        to = lax.rem(mine + d, group)
+        pltpu.make_async_remote_copy(
+            src_ref=buf.at[k, lax.rem(to, secs)], dst_ref=in_a.at[k, lax.rem(mine + group - d, group)],
+            send_sem=a_send.at[k, d - 1], recv_sem=a_recv.at[k, d - 1],
+            device_id=(line * pair + to // secs, lax.rem(to, secs)),
+            device_id_type=MESH).wait_recv()
+
+    def send_b(k, d, slot):
+        to = lax.rem(line + d, rows_of)
         return pltpu.make_async_remote_copy(
-            src_ref=tot.at[k, m], dst_ref=in_b.at[k, dp, m], send_sem=b_send.at[k, m],
-            recv_sem=b_recv.at[k, lax.rem(to - dp + dps - 1, dps)],
-            device_id=(to, sec), device_id_type=MESH)
-
-    def wait_tile(k, m, d):
-        pltpu.make_async_remote_copy(
-            src_ref=tot.at[k, m], dst_ref=in_b.at[k, lax.rem(dp - d + dps, dps), m],
-            send_sem=b_send.at[k, m], recv_sem=b_recv.at[k, d - 1],
-            device_id=(lax.rem(dp + d, dps), sec), device_id_type=MESH).wait_recv()
-
-    def send_all(k, d):
-        to = lax.rem(dp + d, dps)
-        return pltpu.make_async_remote_copy(
-            src_ref=tot.at[k], dst_ref=in_b.at[k, dp], send_sem=b_send.at[k, d - 1],
-            recv_sem=b_recv.at[k, d - 1], device_id=(to, sec), device_id_type=MESH)
-
-    def send_c(k, m, d):
-        return pltpu.make_async_remote_copy(
-            src_ref=fin.at[k, m], dst_ref=fin.at[k, m], send_sem=c_send.at[k, d - 1],
-            recv_sem=c_recv.at[k, m], device_id=(lax.rem(dp + d, dps), sec),
+            src_ref=in_b.at[k, line], dst_ref=in_b.at[k, slot], send_sem=b_send.at[k, d - 1],
+            recv_sem=b_recv.at[k, d - 1], device_id=(to * pair + side_of, sec),
             device_id_type=MESH)
-
-    def each_dp(act):
-        def step(d, carry):
-            act(d)
-            return carry
-        lax.fori_loop(1, dps, step, 0)
 
     def resplit(v):
         whole = v[0:8] + v[8:16]
@@ -104,58 +91,29 @@
         return jnp.where(low, v, jnp.concatenate([top, whole - top], axis=0))
 
     def start_a(k):
-        for d in range(1, secs):
+        for d in range(1, group):
             send_a(k, d).start()
-        in_a[k, sec] = buf[k, sec]
+        in_a[k, mine] = buf[k, sec]
+
+    def add_up(ref, k, m, n):
+        v = ref[k, 0, m].astype(F32)
+        if n <= 8:
+            for p in range(1, n):
+                v = v + ref[k, p, m].astype(F32)
+            return v
+        return lax.fori_loop(1, n, lambda p, acc: acc + ref[k, p, m].astype(F32), v)
 
     def start_b(k):
-        for d in range(1, secs):
-            send_a(k, d).wait_recv()
+        for d in range(1, group):
+            wait_a(k, d)
         for m in range(TILES):
-            v = in_a[k, 0, m].astype(F32)
-            for q in range(1, secs):
-                v = v + in_a[k, q, m].astype(F32)
-            tot[k, m] = (resplit(v) if m == TILES - 1 else v).astype(BF16)
-        if k in DIRECT:
-            each_dp(lambda d: send_all(k, d).start())
-            in_b[k, dp] = tot[k]
-            return
-        for m in range(TILES):
-            @pl.when(dp != owner(k, m, dps))
-            def _():
-                send_tile(k, m).start()
-
-            @pl.when(dp == owner(k, m, dps))
-            def _():
-                in_b[k, dp, m] = tot[k, m]
-
-    def sum_b(k, m):
-        v = lax.fori_loop(1, dps, lambda p, acc: acc + in_b[k, p, m].astype(F32),
-                          in_b[k, 0, m].astype(F32))
-        fin[k, m] = (resplit(v) if m == TILES - 1 else v).astype(BF16)
-
-    def start_c(k):
-        for m in range(TILES):
-            @pl.when(dp == owner(k, m, dps))
-            def _():
-                each_dp(lambda d: wait_tile(k, m, d))
-                sum_b(k, m)
-                each_dp(lambda d: send_c(k, m, d).start())
+            v = add_up(in_a, k, m, group)
+            in_b[k, line, m] = (resplit(v) if m == TILES - 1 else v).astype(BF16)
+        each(rows_of, lambda d: send_b(k, d, line).start())
 
     def finish(k):
-        if k in DIRECT:
-            each_dp(lambda d: pltpu.make_async_remote_copy(
-                src_ref=tot.at[k], dst_ref=in_b.at[k, lax.rem(dp - d + dps, dps)],
-                send_sem=b_send.at[k, d - 1], recv_sem=b_recv.at[k, d - 1],
-                device_id=(lax.rem(dp + d, dps), sec), device_id_type=MESH).wait_recv())
-            for m in range(TILES):
-                sum_b(k, m)
-        else:
-            for m in range(TILES):
-                @pl.when(dp != owner(k, m, dps))
-                def _():
-                    send_c(k, m, 1).wait_recv()
-        rows = [fin[k, m].astype(F32) for m in range(TILES)]
+        each(rows_of, lambda d: send_b(k, d, lax.rem(line + rows_of - d, rows_of)).wait_recv())
+        rows = [add_up(in_b, k, m, rows_of) for m in range(TILES)]
         side = pltpu.roll(rows[-1][0:8] + rows[-1][8:16], 64, 1)[:, 0:64]
         conv_out[k] = (jnp.concatenate(rows[:-1] + [rows[-1][:, 0:64]], axis=1)
                        + prior_precision * own[k])
@@ -274,7 +232,8 @@
     pooled = zero_sum
     for k in range(6):
         b, j = k // 2, k % 2
-        spread(k)
+        if k == 0:
+            spread(0)
 
         def keep(y, out, energy):
             zs[k, y] = out
@@ -298,7 +257,9 @@
                 return carry
             return carry + jnp.sum(out.astype(BF16).astype(F32), axis=0)
 
-        pooled = lax.fori_loop(0, 8, activate, pooled)
+        if k < 5:
+            spread(k + 1)
+        pooled = lax.fori_loop(0, 8, activate, pooled, unroll=8)
 
     pooled = both(pooled) * (1.0 / 64)
     hw2[...] = jnp.zeros((128, 128), F32)
@@ -331,7 +292,7 @@
 
     def advance(k):
         for act, other in AFTER.get(k, ()):
-            {"b": start_b, "c": start_c}[act](other)
+            {"b": start_b, "f": finish}[act](other)
 
     def tally(k, y, d, sums):
         return (sums[0] + over_pairs(d * zs[k, y]), sums[1] + over_pairs(d))
@@ -413,30 +374,22 @@
             advance(k)
 
     for act, k in TAIL:
-        {"b": start_b, "c": start_c, "f": finish}[act](k)
+        {"b": start_b, "f": finish}[act](k)
     for k in range(6):
         for d in range(1, secs):
             send_w(k, d).wait_send()
     for k in range(6):
-        for d in range(1, secs):
+        for d in range(1, group):
             send_a(k, d).wait_send()
-        if k in DIRECT:
-            each_dp(lambda d: send_all(k, d).wait_send())
-            continue
-        for m in range(TILES):
-            @pl.when(dp != owner(k, m, dps))
-            def _():
-                send_tile(k, m).wait_send()
-
-            @pl.when(dp == owner(k, m, dps))
-            def _():
-                each_dp(lambda d: send_c(k, m, d).wait_send())
+        each(rows_of, lambda d: send_b(k, d, line).wait_send())
 
 
 def all_grads(total, dps, secs, images_in, labels, own, gain, bias, hw, hb):
     vmem = pl.BlockSpec(memory_space=pltpu.VMEM)
     hbm = pl.BlockSpec(memory_space=pltpu.HBM)
     dma = pltpu.SemaphoreType.DMA
+    pair = 2 if dps % 2 == 0 else 1
+    group = pair * secs
     return pl.pallas_call(
         functools.partial(kernel, total, dps, secs),
         out_shape=(jax.ShapeDtypeStruct(own.shape, F32),
@@ -460,17 +413,14 @@
             pltpu.VMEM((8, 128), jnp.int32),
             pltpu.VMEM((secs,) + own.shape, BF16),
             pltpu.VMEM((6, secs, TILES, 16, 128), BF16),
-            pltpu.VMEM((6, secs, TILES, 16, 128), BF16),
-            pltpu.VMEM((6, TILES, 16, 128), BF16),
-            pltpu.VMEM((6, dps, TILES, 16, 128), BF16),
-            pltpu.VMEM((6, TILES, 16, 128), BF16),
+            pltpu.VMEM((6, group, TILES, 16, 128), BF16),
+            pltpu.VMEM((6, dps // pair, TILES, 16, 128), BF16),
             pltpu.VMEM(images_in.shape, BF16),
             pltpu.VMEM(own.shape, F32),
             dma((2,)),
             dma((6, secs - 1)), dma((6, secs - 1)),
-            dma((6, secs - 1)), dma((6, secs - 1)),
-            dma((6, max(dps - 1, TILES))), dma((6, dps)),
-            dma((6, dps)), dma((6, TILES)),
+            dma((6, group - 1)), dma((6, group - 1)),
+            dma((6, dps // pair - 1)), dma((6, dps // pair - 1)),
         ],
         compiler_params=pltpu.CompilerParams(
             vmem_limit_bytes=63 * 1024 * 1024 + 768 * 1024, collective_id=0, has_side_effects=True),

time: 46.9 us -> 42.3 us (0.902)
  Pallas kernels: 46 us -> 41.4 us
    pallas_call x1, Pallas kernels: 44.3 us -> 39.8 us  [all_grads(): pl.pallas_call(functools.partial(kernel, total, dps, secs), out_shape=(ja...]
where the time goes in v4:
time: 42.3 us; the launch traced here: 42.1 us
  Pallas kernels  41.4 us (98%)
  between operations  0.64 us (2%)
    pallas_call x1, Pallas kernels, all_grads(): pl.pallas_call(functools.partial(kernel, total, dps, secs), out_shape=(ja...  39.8 us
    pallas_call x1, Pallas kernels, outputs(): pl.pallas_call(hand_over, out_shape=tuple((jax.ShapeDtypeStruct(v.shape,...  1.68 us

profile of v4, /device:TPU:0, one launch (start us, length us, event | category | flops | bytes accessed | tf_op | source)
XLA Modules:
  0.0 42.1 jit_solution(14587139237672924811)
XLA Ops:
  0.6 39.8 %shard_map.102 = (f32[6,16,576]{2,1,0:T(8,128)}, f32[3,2,2,64]{3,2,1,0:T(2,128)}, f32[10,64]{1,0:T(8,128)}, f32[1,10]{1,0:T(1,128)}) custom-call(bf16[64,4096]{1,0:T(8,128)(2,1)} %img_hbm.1, s32[1,64]{1,0:T(1,128)} %bitcast.13, f32[6,16,576]{2,1,0:T(8,128)} %bitcast.11, f32[3,2,64]{2,1,0:T(2,128)} %gain.1, f32[3,2,64]{2,1,0:T(2,128)} %bias.1, ...), custom_call_target="tpu_custom_call" | custom-call | tf_op jit(solution)/shard_map/pallas_call | solution.py:393
  40.4 1.7 %shard_map.103 = (f32[6,16,576]{2,1,0:T(8,128)}, f32[3,2,2,64]{3,2,1,0:T(2,128)}, f32[10,64]{1,0:T(8,128)}, f32[1,10]{1,0:T(1,128)}) custom-call(f32[6,16,576]{2,1,0:T(8,128)} %get-tuple-element.12.refs_0_, f32[3,2,2,64]{3,2,1,0:T(2,128)} %get-tuple-element.13.refs_1_, f32[10,64]{1,0:T(8,128)} %get-tuple-element.14.refs_2_, f32[1,10]{1,0:T(1,128)} %get-tuple-element.15.refs_3_), custom_call_target="tpu_custom_call" | custom-call | tf_op jit(solution)/shard_map/pallas_call | solution.py:438

commit v5 on v4

--- a/solution.py
+++ b/solution.py
@@ -16,9 +16,8 @@
 
 
 TILES = 5
-AFTER = {1: (("b", 5),)}
-TAIL = (("b", 4), ("b", 3), ("b", 2), ("b", 1), ("f", 5), ("b", 0), ("f", 4), ("f", 3),
-        ("f", 2), ("f", 1), ("f", 0))
+AFTER = {2: (("b", 5),), 1: (("b", 4),)}
+TAIL = (("b", 3), ("b", 2), ("b", 1), ("f", 5), ("b", 0), ("f", 4), ("f", 3), ("f", 2), ("f", 1), ("f", 0))
 
 
 def kernel(total, dps, secs, img_hbm, labels, own_hbm, gain, bias, hw, hb,

time: 42.3 us -> 40.5 us (0.957)
  Pallas kernels: 41.4 us -> 39.7 us
    pallas_call x1, Pallas kernels: 39.8 us -> 38 us  [all_grads(): pl.pallas_call(functools.partial(kernel, total, dps, secs), out_shape=(ja...]
where the time goes in v5:
time: 40.5 us; the launch traced here: 40.3 us
  Pallas kernels  39.7 us (98%)
  between operations  0.64 us (2%)
    pallas_call x1, Pallas kernels, all_grads(): pl.pallas_call(functools.partial(kernel, total, dps, secs), out_shape=(ja...  38 us
    pallas_call x1, Pallas kernels, outputs(): pl.pallas_call(hand_over, out_shape=tuple((jax.ShapeDtypeStruct(v.shape,...  1.68 us

profile of v5, /device:TPU:0, one launch (start us, length us, event | category | flops | bytes accessed | tf_op | source)
XLA Modules:
  0.0 40.3 jit_solution(16627804048116177105)
XLA Ops:
  0.6 38.0 %shard_map.102 = (f32[6,16,576]{2,1,0:T(8,128)}, f32[3,2,2,64]{3,2,1,0:T(2,128)}, f32[10,64]{1,0:T(8,128)}, f32[1,10]{1,0:T(1,128)}) custom-call(bf16[64,4096]{1,0:T(8,128)(2,1)} %img_hbm.1, s32[1,64]{1,0:T(1,128)} %bitcast.13, f32[6,16,576]{2,1,0:T(8,128)} %bitcast.11, f32[3,2,64]{2,1,0:T(2,128)} %gain.1, f32[3,2,64]{2,1,0:T(2,128)} %bias.1, ...), custom_call_target="tpu_custom_call" | custom-call | tf_op jit(solution)/shard_map/pallas_call | solution.py:392
  38.6 1.7 %shard_map.103 = (f32[6,16,576]{2,1,0:T(8,128)}, f32[3,2,2,64]{3,2,1,0:T(2,128)}, f32[10,64]{1,0:T(8,128)}, f32[1,10]{1,0:T(1,128)}) custom-call(f32[6,16,576]{2,1,0:T(8,128)} %get-tuple-element.12.refs_0_, f32[3,2,2,64]{3,2,1,0:T(2,128)} %get-tuple-element.13.refs_1_, f32[10,64]{1,0:T(8,128)} %get-tuple-element.14.refs_2_, f32[1,10]{1,0:T(1,128)} %get-tuple-element.15.refs_3_), custom_call_target="tpu_custom_call" | custom-call | tf_op jit(solution)/shard_map/pallas_call | solution.py:437

commit v6 on v5

--- a/solution.py
+++ b/solution.py
@@ -16,8 +16,8 @@
 
 
 TILES = 5
-AFTER = {2: (("b", 5),), 1: (("b", 4),)}
-TAIL = (("b", 3), ("b", 2), ("b", 1), ("f", 5), ("b", 0), ("f", 4), ("f", 3), ("f", 2), ("f", 1), ("f", 0))
+AFTER = {3: (("b", 5),), 2: (("b", 4),), 1: (("b", 3),)}
+TAIL = (("b", 2), ("b", 1), ("f", 5), ("b", 0), ("f", 4), ("f", 3), ("f", 2), ("f", 1))
 
 
 def kernel(total, dps, secs, img_hbm, labels, own_hbm, gain, bias, hw, hb,
@@ -377,10 +377,12 @@
     for k in range(6):
         for d in range(1, secs):
             send_w(k, d).wait_send()
-    for k in range(6):
         for d in range(1, group):
             send_a(k, d).wait_send()
-        each(rows_of, lambda d: send_b(k, d, line).wait_send())
+        if k > 0:
+            each(rows_of, lambda d: send_b(k, d, line).wait_send())
+    finish(0)
+    each(rows_of, lambda d: send_b(0, d, line).wait_send())
 
 
 def all_grads(total, dps, secs, images_in, labels, own, gain, bias, hw, hb):

time: 40.5 us -> 38.9 us (0.960)
  Pallas kernels: 39.7 us -> 38.1 us
    pallas_call x1, Pallas kernels: 38 us -> 36.4 us  [all_grads(): pl.pallas_call(functools.partial(kernel, total, dps, secs), out_shape=(ja...]
where the time goes in v6:
time: 38.9 us; the launch traced here: 38.7 us
  Pallas kernels  38.1 us (98%)
  between operations  0.64 us (2%)
    pallas_call x1, Pallas kernels, all_grads(): pl.pallas_call(functools.partial(kernel, total, dps, secs), out_shape=(ja...  36.4 us
    pallas_call x1, Pallas kernels, outputs(): pl.pallas_call(hand_over, out_shape=tuple((jax.ShapeDtypeStruct(v.shape,...  1.68 us

profile of v6, /device:TPU:0, one launch (start us, length us, event | category | flops | bytes accessed | tf_op | source)
XLA Modules:
  0.0 38.7 jit_solution(14259741652518558182)
XLA Ops:
  0.6 36.4 %shard_map.102 = (f32[6,16,576]{2,1,0:T(8,128)}, f32[3,2,2,64]{3,2,1,0:T(2,128)}, f32[10,64]{1,0:T(8,128)}, f32[1,10]{1,0:T(1,128)}) custom-call(bf16[64,4096]{1,0:T(8,128)(2,1)} %img_hbm.1, s32[1,64]{1,0:T(1,128)} %bitcast.13, f32[6,16,576]{2,1,0:T(8,128)} %bitcast.11, f32[3,2,64]{2,1,0:T(2,128)} %gain.1, f32[3,2,64]{2,1,0:T(2,128)} %bias.1, ...), custom_call_target="tpu_custom_call" | custom-call | tf_op jit(solution)/shard_map/pallas_call | solution.py:394
  37.1 1.7 %shard_map.103 = (f32[6,16,576]{2,1,0:T(8,128)}, f32[3,2,2,64]{3,2,1,0:T(2,128)}, f32[10,64]{1,0:T(8,128)}, f32[1,10]{1,0:T(1,128)}) custom-call(f32[6,16,576]{2,1,0:T(8,128)} %get-tuple-element.12.refs_0_, f32[3,2,2,64]{3,2,1,0:T(2,128)} %get-tuple-element.13.refs_1_, f32[10,64]{1,0:T(8,128)} %get-tuple-element.14.refs_2_, f32[1,10]{1,0:T(1,128)} %get-tuple-element.15.refs_3_), custom_call_target="tpu_custom_call" | custom-call | tf_op jit(solution)/shard_map/pallas_call | solution.py:439
